TPU v7x, 512 devices: a whole 4x4x16 slice. The times are simulated.
512 devices in a mesh: gx: 16 (over y, z_lo), gy: 32 (over x, z_hi, core).
Axes of the slice: x: 4, y: 4, z: 16 (z_hi: 4, z_lo: 4; z = z_hi * 4 + z_lo), core: 2. Of those that a mesh axis runs over, the one named last changes fastest.
Arguments:
- impedance: bfloat16 [16, 32, 2, 1024, 1024], P('gx', 'gy'), may hold values from -0.1875 to 0.1875
- sources: bfloat16 [16, 32, 2, 48, 1024], P('gx', 'gy'), may hold values from -6 to 6
- pattern: int32 [16, 32, 2, 2], P('gx', 'gy'), may hold values from 0 to 7
Outputs:
- combined: bfloat16 [16, 32, 2, 48, 1024], P('gx', 'gy')
All inputs are finite; a program needn't handle non-finite values.
Results may differ from a plain program's by a relative error of at most 0.02.
Values sent between devices are 32-bit elements; how exact they have to be, the bound alone decides.
A program may use at most 64 MiB of HBM per device.

v0:
```python
import jax
import jax.numpy as jnp
from jax import lax
from jax.sharding import PartitionSpec as P

COUPLING = 0.5


def shifted(value, axis, steps):
    count = lax.axis_size(axis)
    leading, last = (max(0, -steps), min(count, count - steps))
    return lax.ppermute(value, axis, [(source, source + steps) for source in range(leading, last)])


def rotate(code, real_in, imag_in):
    conj_sign = jnp.where(code >= 4, -1.0, 1.0)
    quarter = code % 4
    cos_part = jnp.where(quarter == 0, 1.0, jnp.where(quarter == 2, -1.0, 0.0))
    sine_part = jnp.where(quarter == 1, 1.0, jnp.where(quarter == 3, -1.0, 0.0))
    imag_flip = conj_sign * imag_in
    return (cos_part * real_in - sine_part * imag_flip, sine_part * real_in + cos_part * imag_flip)


def apply_operator(left_in, down_in, edge_codes, operator_block, source_block, transpose):
    left_re, left_im = rotate(edge_codes[0], left_in[0], left_in[1])
    down_re, down_im = rotate(edge_codes[1], down_in[0], down_in[1])
    blended = jnp.concatenate([left_re + down_re, left_im + down_im], axis=0).astype(jnp.bfloat16)
    contract = (((1,), (1,)), ((), ())) if transpose else (((1,), (0,)), ((), ()))
    real_part = lax.dot_general(
        blended, operator_block[0], contract, preferred_element_type=jnp.float32
    )
    imag_part = lax.dot_general(
        blended, operator_block[1], contract, preferred_element_type=jnp.float32
    )
    half_rows = blended.shape[0] // 2
    out_re = real_part[:half_rows] - imag_part[half_rows:]
    out_im = imag_part[:half_rows] + real_part[half_rows:]
    return source_block.astype(jnp.float32) + COUPLING * jnp.stack([out_re, out_im])


def forward_links(latest):
    left_in = shifted(latest, "gx", 1)
    down_in = shifted(latest, "gy", 1)
    return (left_in, down_in)


def reverse_links(latest):
    left_in = shifted(latest, "gx", -1)
    down_in = shifted(latest, "gy", -1)
    return (left_in, down_in)


def per_device(impedance, sources, pattern):
    operator_block = impedance[0, 0]
    local_source = sources[0, 0]
    code_table = pattern[0, 0]
    count_cols = lax.axis_size("gx")
    count_rows = lax.axis_size("gy")
    col_index = lax.axis_index("gx")
    row_index = lax.axis_index("gy")
    depth_fwd = col_index + row_index
    depth_rev = count_cols - 1 - col_index + (count_rows - 1 - row_index)
    rhs_count = local_source.shape[1]
    trace_width = local_source.shape[2]
    block_rows = 6
    groups = rhs_count // block_rows
    sections = count_cols + count_rows - 1 + groups - 1

    def advance(section, state_pair, left_in, down_in, depth_now, direction):
        totals, latest = state_pair
        group_index = section - depth_now

        def compute():
            offset = group_index * block_rows
            source_block = lax.dynamic_slice_in_dim(local_source, offset, block_rows, 1)
            update = apply_operator(
                left_in,
                down_in,
                code_table[direction],
                operator_block,
                source_block,
                direction == 1,
            )
            return (lax.dynamic_update_slice_in_dim(totals, update, offset, 1), update)

        def retain():
            return (totals, latest)

        active = (group_index >= 0) & (group_index < groups)
        return lax.cond(active, compute, retain)

    initial = (
        jnp.zeros((2, rhs_count, trace_width), jnp.float32),
        jnp.zeros((2, block_rows, trace_width), jnp.float32),
    )

    def both_sweeps(section, state_both):
        forward, reverse = state_both
        fwd_left, fwd_down = forward_links(forward[1])
        rev_left, rev_down = reverse_links(reverse[1])
        return (
            advance(section, forward, fwd_left, fwd_down, depth_fwd, 0),
            advance(section, reverse, rev_left, rev_down, depth_rev, 1),
        )

    forward, reverse = lax.fori_loop(0, sections, both_sweeps, (initial, initial))
    return (forward[0] + reverse[0]).astype(jnp.bfloat16)[None, None]


def solution(mesh):
    in_specs = (
        P("gx", "gy", None, None, None),
        P("gx", "gy", None, None, None),
        P("gx", "gy", None, None),
    )
    out_specs = P("gx", "gy", None, None, None)
    return jax.shard_map(
        per_device, mesh=mesh, in_specs=in_specs, out_specs=out_specs, check_vma=False
    )
```

profile of v0, /device:TPU:1, one launch (start us, length us, event | category | flops | bytes accessed | tf_op | source)
XLA Modules:
  0.0 1804.9 jit_solution(8919845993116470969)
XLA Ops:
  1.3 1802.9 %while.19 = (s32[]{:T(128)}, f32[2,48,1024]{2,1,0:T(8,128)S(1)}, f32[2,6,1024]{2,1,0:T(8,128)}, f32[2,48,1024]{2,1,0:T(8,128)S(1)}, f32[2,6,1024]{2,1,0:T(8,128)...) while((s32[]{:T(128)}, f32[2,48,1024]{2,1,0:T(8,128)S(1)}, ...), condition=%wide.region_5.6_spmd, body=%wide.region_0.5_spmd.sunk | while | flops 101204056 | bytes 10454609 | solution.py:106
  821.4 17.7 collective-permute-done.3
  839.1 22.4 %collective-permute-start.1 = (f32[2,6,1024]{2,1,0:T(8,128)}, f32[2,6,1024]{2,1,0:T(8,128)S(1)}, u32[]{:S(2)}, u32[]{:S(2)}) collective-permute-start(f32[2,6,1024]{2,1,0:T(8,128)} %get-tuple-element.363), channel_id=1, source_target_pairs={{0,1},{1,2},{2,3},{3,4},{4,5},{5,6},{6,7},{7,8},{8,9},{9,10},{10,1... | collective-permute-start | bytes 147464 | tf_op jit(solution)/shard_map/while/body/eval_jaxpr/ppermute | solution.py:12
  871.1 28.8 %collective-permute-done.3 = f32[2,6,1024]{2,1,0:T(8,128)S(1)} collective-permute-done((f32[2,6,1024]{2,1,0:T(8,128)}, f32[2,6,1024]{2,1,0:T(8,128)S(1)}, u32[]{:S(2)}, u32[]{:S(2)}) %collective-permute-start.3) | collective-permute-done | bytes 49184 | tf_op jit(solution)/shard_map/while/body/eval_jaxpr/ppermute | solution.py:12
  914.5 20.2 %collective-permute-start = (f32[2,6,1024]{2,1,0:T(8,128)}, f32[2,6,1024]{2,1,0:T(8,128)S(1)}, u32[]{:S(2)}, u32[]{:S(2)}) collective-permute-start(f32[2,6,1024]{2,1,0:T(8,128)} %get-tuple-element.363), channel_id=1, source_target_pairs={{0,32},{32,64},{64,96},{96,128},{128,160},{160,192},{192,224},{224... | collective-permute-start | bytes 147464 | tf_op jit(solution)/shard_map/while/body/eval_jaxpr/ppermute | solution.py:12
  951.5 22.7 %collective-permute-start.1 = (f32[2,6,1024]{2,1,0:T(8,128)}, f32[2,6,1024]{2,1,0:T(8,128)S(1)}, u32[]{:S(2)}, u32[]{:S(2)}) collective-permute-start(f32[2,6,1024]{2,1,0:T(8,128)} %get-tuple-element.363), channel_id=1, source_target_pairs={{0,1},{1,2},{2,3},{3,4},{4,5},{5,6},{6,7},{7,8},{8,9},{9,10},{10,1... | collective-permute-start | bytes 147464 | tf_op jit(solution)/shard_map/while/body/eval_jaxpr/ppermute | solution.py:12
  983.0 21.3 %collective-permute-done.3 = f32[2,6,1024]{2,1,0:T(8,128)S(1)} collective-permute-done((f32[2,6,1024]{2,1,0:T(8,128)}, f32[2,6,1024]{2,1,0:T(8,128)S(1)}, u32[]{:S(2)}, u32[]{:S(2)}) %collective-permute-start.3) | collective-permute-done | bytes 49184 | tf_op jit(solution)/shard_map/while/body/eval_jaxpr/ppermute | solution.py:12
  1019.4 20.3 %collective-permute-start = (f32[2,6,1024]{2,1,0:T(8,128)}, f32[2,6,1024]{2,1,0:T(8,128)S(1)}, u32[]{:S(2)}, u32[]{:S(2)}) collective-permute-start(f32[2,6,1024]{2,1,0:T(8,128)} %get-tuple-element.363), channel_id=1, source_target_pairs={{0,32},{32,64},{64,96},{96,128},{128,160},{160,192},{192,224},{224... | collective-permute-start | bytes 147464 | tf_op jit(solution)/shard_map/while/body/eval_jaxpr/ppermute | solution.py:12
  1050.8 21.4 %collective-permute-start.1 = (f32[2,6,1024]{2,1,0:T(8,128)}, f32[2,6,1024]{2,1,0:T(8,128)S(1)}, u32[]{:S(2)}, u32[]{:S(2)}) collective-permute-start(f32[2,6,1024]{2,1,0:T(8,128)} %get-tuple-element.363), channel_id=1, source_target_pairs={{0,1},{1,2},{2,3},{3,4},{4,5},{5,6},{6,7},{7,8},{8,9},{9,10},{10,1... | collective-permute-start | bytes 147464 | tf_op jit(solution)/shard_map/while/body/eval_jaxpr/ppermute | solution.py:12
  1088.4 21.5 %collective-permute-done.3 = f32[2,6,1024]{2,1,0:T(8,128)S(1)} collective-permute-done((f32[2,6,1024]{2,1,0:T(8,128)}, f32[2,6,1024]{2,1,0:T(8,128)S(1)}, u32[]{:S(2)}, u32[]{:S(2)}) %collective-permute-start.3) | collective-permute-done | bytes 49184 | tf_op jit(solution)/shard_map/while/body/eval_jaxpr/ppermute | solution.py:12
  1118.7 15.2 collective-permute-start
  1137.3 18.5 %collective-permute-done.3 = f32[2,6,1024]{2,1,0:T(8,128)S(1)} collective-permute-done((f32[2,6,1024]{2,1,0:T(8,128)}, f32[2,6,1024]{2,1,0:T(8,128)S(1)}, u32[]{:S(2)}, u32[]{:S(2)}) %collective-permute-start.3) | collective-permute-done | bytes 49184 | tf_op jit(solution)/shard_map/while/body/eval_jaxpr/ppermute | solution.py:12
  1155.7 23.3 %collective-permute-start.1 = (f32[2,6,1024]{2,1,0:T(8,128)}, f32[2,6,1024]{2,1,0:T(8,128)S(1)}, u32[]{:S(2)}, u32[]{:S(2)}) collective-permute-start(f32[2,6,1024]{2,1,0:T(8,128)} %get-tuple-element.363), channel_id=1, source_target_pairs={{0,1},{1,2},{2,3},{3,4},{4,5},{5,6},{6,7},{7,8},{8,9},{9,10},{10,1... | collective-permute-start | bytes 147464 | tf_op jit(solution)/shard_map/while/body/eval_jaxpr/ppermute | solution.py:12
  1186.0 22.9 %collective-permute-done.3 = f32[2,6,1024]{2,1,0:T(8,128)S(1)} collective-permute-done((f32[2,6,1024]{2,1,0:T(8,128)}, f32[2,6,1024]{2,1,0:T(8,128)S(1)}, u32[]{:S(2)}, u32[]{:S(2)}) %collective-permute-start.3) | collective-permute-done | bytes 49184 | tf_op jit(solution)/shard_map/while/body/eval_jaxpr/ppermute | solution.py:12
  1208.9 15.7 collective-permute-start.1
  1224.7 15.5 collective-permute-start
  1255.7 18.8 %collective-permute-start.1 = (f32[2,6,1024]{2,1,0:T(8,128)}, f32[2,6,1024]{2,1,0:T(8,128)S(1)}, u32[]{:S(2)}, u32[]{:S(2)}) collective-permute-start(f32[2,6,1024]{2,1,0:T(8,128)} %get-tuple-element.363), channel_id=1, source_target_pairs={{0,1},{1,2},{2,3},{3,4},{4,5},{5,6},{6,7},{7,8},{8,9},{9,10},{10,1... | collective-permute-start | bytes 147464 | tf_op jit(solution)/shard_map/while/body/eval_jaxpr/ppermute | solution.py:12
  1280.8 25.8 %collective-permute-done.3 = f32[2,6,1024]{2,1,0:T(8,128)S(1)} collective-permute-done((f32[2,6,1024]{2,1,0:T(8,128)}, f32[2,6,1024]{2,1,0:T(8,128)S(1)}, u32[]{:S(2)}, u32[]{:S(2)}) %collective-permute-start.3) | collective-permute-done | bytes 49184 | tf_op jit(solution)/shard_map/while/body/eval_jaxpr/ppermute | solution.py:12
  1341.4 17.6 collective-permute-start.1
  1365.7 24.6 %collective-permute-done.3 = f32[2,6,1024]{2,1,0:T(8,128)S(1)} collective-permute-done((f32[2,6,1024]{2,1,0:T(8,128)}, f32[2,6,1024]{2,1,0:T(8,128)S(1)}, u32[]{:S(2)}, u32[]{:S(2)}) %collective-permute-start.3) | collective-permute-done | bytes 49184 | tf_op jit(solution)/shard_map/while/body/eval_jaxpr/ppermute | solution.py:12
  1426.2 18.5 %collective-permute-start.1 = (f32[2,6,1024]{2,1,0:T(8,128)}, f32[2,6,1024]{2,1,0:T(8,128)S(1)}, u32[]{:S(2)}, u32[]{:S(2)}) collective-permute-start(f32[2,6,1024]{2,1,0:T(8,128)} %get-tuple-element.363), channel_id=1, source_target_pairs={{0,1},{1,2},{2,3},{3,4},{4,5},{5,6},{6,7},{7,8},{8,9},{9,10},{10,1... | collective-permute-start | bytes 147464 | tf_op jit(solution)/shard_map/while/body/eval_jaxpr/ppermute | solution.py:12
  1451.1 25.8 %collective-permute-done.3 = f32[2,6,1024]{2,1,0:T(8,128)S(1)} collective-permute-done((f32[2,6,1024]{2,1,0:T(8,128)}, f32[2,6,1024]{2,1,0:T(8,128)S(1)}, u32[]{:S(2)}, u32[]{:S(2)}) %collective-permute-start.3) | collective-permute-done | bytes 49184 | tf_op jit(solution)/shard_map/while/body/eval_jaxpr/ppermute | solution.py:12
  1482.9 15.5 collective-permute-start
  1511.3 20.0 %collective-permute-start.1 = (f32[2,6,1024]{2,1,0:T(8,128)}, f32[2,6,1024]{2,1,0:T(8,128)S(1)}, u32[]{:S(2)}, u32[]{:S(2)}) collective-permute-start(f32[2,6,1024]{2,1,0:T(8,128)} %get-tuple-element.363), channel_id=1, source_target_pairs={{0,1},{1,2},{2,3},{3,4},{4,5},{5,6},{6,7},{7,8},{8,9},{9,10},{10,1... | collective-permute-start | bytes 147464 | tf_op jit(solution)/shard_map/while/body/eval_jaxpr/ppermute | solution.py:12
  (634 shorter events, 1457.4 us)
Async XLA Ops:
  839.1 31.9 %collective-permute-start.1 = (f32[2,6,1024]{2,1,0:T(8,128)}, f32[2,6,1024]{2,1,0:T(8,128)S(1)}, u32[]{:S(2)}, u32[]{:S(2)}) collective-permute-start(f32[2,6,1024]{2,1,0:T(8,128)} %get-tuple-element.363), channel_id=1, source_target_pairs={{0,1},{1,2},{2,3},{3,4},{4,5},{5,6},{6,7},{7,8},{8,9},{9,10},{10,1... | collective-permute-start | bytes 147464 | tf_op jit(solution)/shard_map/while/body/eval_jaxpr/ppermute | solution.py:12
  867.8 32.1 %collective-permute-start.3 = (f32[2,6,1024]{2,1,0:T(8,128)}, f32[2,6,1024]{2,1,0:T(8,128)S(1)}, u32[]{:S(2)}, u32[]{:S(2)}) collective-permute-start(f32[2,6,1024]{2,1,0:T(8,128)} %get-tuple-element.365), channel_id=1, source_target_pairs={{1,0},{2,1},{3,2},{4,3},{5,4},{6,5},{7,6},{8,7},{9,8},{10,9},{11,1... | collective-permute-start | bytes 147464 | tf_op jit(solution)/shard_map/while/body/eval_jaxpr/ppermute | solution.py:12
  869.7 30.2 %collective-permute-start.2 = (f32[2,6,1024]{2,1,0:T(8,128)}, f32[2,6,1024]{2,1,0:T(8,128)S(1)}, u32[]{:S(2)}, u32[]{:S(2)}) collective-permute-start(f32[2,6,1024]{2,1,0:T(8,128)} %get-tuple-element.365), channel_id=1, source_target_pairs={{32,0},{64,32},{96,64},{128,96},{160,128},{192,160},{224,192},{256... | collective-permute-start | bytes 147464 | tf_op jit(solution)/shard_map/while/body/eval_jaxpr/ppermute | solution.py:12
  899.9 38.2 %collective-permute-start.1 = (f32[2,6,1024]{2,1,0:T(8,128)}, f32[2,6,1024]{2,1,0:T(8,128)S(1)}, u32[]{:S(2)}, u32[]{:S(2)}) collective-permute-start(f32[2,6,1024]{2,1,0:T(8,128)} %get-tuple-element.363), channel_id=1, source_target_pairs={{0,1},{1,2},{2,3},{3,4},{4,5},{5,6},{6,7},{7,8},{8,9},{9,10},{10,1... | collective-permute-start | bytes 147464 | tf_op jit(solution)/shard_map/while/body/eval_jaxpr/ppermute | solution.py:12
  951.5 31.5 %collective-permute-start.1 = (f32[2,6,1024]{2,1,0:T(8,128)}, f32[2,6,1024]{2,1,0:T(8,128)S(1)}, u32[]{:S(2)}, u32[]{:S(2)}) collective-permute-start(f32[2,6,1024]{2,1,0:T(8,128)} %get-tuple-element.363), channel_id=1, source_target_pairs={{0,1},{1,2},{2,3},{3,4},{4,5},{5,6},{6,7},{7,8},{8,9},{9,10},{10,1... | collective-permute-start | bytes 147464 | tf_op jit(solution)/shard_map/while/body/eval_jaxpr/ppermute | solution.py:12
  979.7 24.6 %collective-permute-start.3 = (f32[2,6,1024]{2,1,0:T(8,128)}, f32[2,6,1024]{2,1,0:T(8,128)S(1)}, u32[]{:S(2)}, u32[]{:S(2)}) collective-permute-start(f32[2,6,1024]{2,1,0:T(8,128)} %get-tuple-element.365), channel_id=1, source_target_pairs={{1,0},{2,1},{3,2},{4,3},{5,4},{6,5},{7,6},{8,7},{9,8},{10,9},{11,1... | collective-permute-start | bytes 147464 | tf_op jit(solution)/shard_map/while/body/eval_jaxpr/ppermute | solution.py:12
  1004.3 38.7 %collective-permute-start.1 = (f32[2,6,1024]{2,1,0:T(8,128)}, f32[2,6,1024]{2,1,0:T(8,128)S(1)}, u32[]{:S(2)}, u32[]{:S(2)}) collective-permute-start(f32[2,6,1024]{2,1,0:T(8,128)} %get-tuple-element.363), channel_id=1, source_target_pairs={{0,1},{1,2},{2,3},{3,4},{4,5},{5,6},{6,7},{7,8},{8,9},{9,10},{10,1... | collective-permute-start | bytes 147464 | tf_op jit(solution)/shard_map/while/body/eval_jaxpr/ppermute | solution.py:12
  1050.8 37.6 %collective-permute-start.1 = (f32[2,6,1024]{2,1,0:T(8,128)}, f32[2,6,1024]{2,1,0:T(8,128)S(1)}, u32[]{:S(2)}, u32[]{:S(2)}) collective-permute-start(f32[2,6,1024]{2,1,0:T(8,128)} %get-tuple-element.363), channel_id=1, source_target_pairs={{0,1},{1,2},{2,3},{3,4},{4,5},{5,6},{6,7},{7,8},{8,9},{9,10},{10,1... | collective-permute-start | bytes 147464 | tf_op jit(solution)/shard_map/while/body/eval_jaxpr/ppermute | solution.py:12
  1085.1 24.8 %collective-permute-start.3 = (f32[2,6,1024]{2,1,0:T(8,128)}, f32[2,6,1024]{2,1,0:T(8,128)S(1)}, u32[]{:S(2)}, u32[]{:S(2)}) collective-permute-start(f32[2,6,1024]{2,1,0:T(8,128)} %get-tuple-element.365), channel_id=1, source_target_pairs={{1,0},{2,1},{3,2},{4,3},{5,4},{6,5},{7,6},{8,7},{9,8},{10,9},{11,1... | collective-permute-start | bytes 147464 | tf_op jit(solution)/shard_map/while/body/eval_jaxpr/ppermute | solution.py:12
  1109.9 27.3 %collective-permute-start.1 = (f32[2,6,1024]{2,1,0:T(8,128)}, f32[2,6,1024]{2,1,0:T(8,128)S(1)}, u32[]{:S(2)}, u32[]{:S(2)}) collective-permute-start(f32[2,6,1024]{2,1,0:T(8,128)} %get-tuple-element.363), channel_id=1, source_target_pairs={{0,1},{1,2},{2,3},{3,4},{4,5},{5,6},{6,7},{7,8},{8,9},{9,10},{10,1... | collective-permute-start | bytes 147464 | tf_op jit(solution)/shard_map/while/body/eval_jaxpr/ppermute | solution.py:12
  1155.7 30.2 %collective-permute-start.1 = (f32[2,6,1024]{2,1,0:T(8,128)}, f32[2,6,1024]{2,1,0:T(8,128)S(1)}, u32[]{:S(2)}, u32[]{:S(2)}) collective-permute-start(f32[2,6,1024]{2,1,0:T(8,128)} %get-tuple-element.363), channel_id=1, source_target_pairs={{0,1},{1,2},{2,3},{3,4},{4,5},{5,6},{6,7},{7,8},{8,9},{9,10},{10,1... | collective-permute-start | bytes 147464 | tf_op jit(solution)/shard_map/while/body/eval_jaxpr/ppermute | solution.py:12
  1182.7 26.2 %collective-permute-start.3 = (f32[2,6,1024]{2,1,0:T(8,128)}, f32[2,6,1024]{2,1,0:T(8,128)S(1)}, u32[]{:S(2)}, u32[]{:S(2)}) collective-permute-start(f32[2,6,1024]{2,1,0:T(8,128)} %get-tuple-element.365), channel_id=1, source_target_pairs={{1,0},{2,1},{3,2},{4,3},{5,4},{6,5},{7,6},{8,7},{9,8},{10,9},{11,1... | collective-permute-start | bytes 147464 | tf_op jit(solution)/shard_map/while/body/eval_jaxpr/ppermute | solution.py:12
  1208.9 34.5 %collective-permute-start.1 = (f32[2,6,1024]{2,1,0:T(8,128)}, f32[2,6,1024]{2,1,0:T(8,128)S(1)}, u32[]{:S(2)}, u32[]{:S(2)}) collective-permute-start(f32[2,6,1024]{2,1,0:T(8,128)} %get-tuple-element.363), channel_id=1, source_target_pairs={{0,1},{1,2},{2,3},{3,4},{4,5},{5,6},{6,7},{7,8},{8,9},{9,10},{10,1... | collective-permute-start | bytes 147464 | tf_op jit(solution)/shard_map/while/body/eval_jaxpr/ppermute | solution.py:12
  1255.7 25.1 %collective-permute-start.1 = (f32[2,6,1024]{2,1,0:T(8,128)}, f32[2,6,1024]{2,1,0:T(8,128)S(1)}, u32[]{:S(2)}, u32[]{:S(2)}) collective-permute-start(f32[2,6,1024]{2,1,0:T(8,128)} %get-tuple-element.363), channel_id=1, source_target_pairs={{0,1},{1,2},{2,3},{3,4},{4,5},{5,6},{6,7},{7,8},{8,9},{9,10},{10,1... | collective-permute-start | bytes 147464 | tf_op jit(solution)/shard_map/while/body/eval_jaxpr/ppermute | solution.py:12
  1277.5 29.1 %collective-permute-start.3 = (f32[2,6,1024]{2,1,0:T(8,128)}, f32[2,6,1024]{2,1,0:T(8,128)S(1)}, u32[]{:S(2)}, u32[]{:S(2)}) collective-permute-start(f32[2,6,1024]{2,1,0:T(8,128)} %get-tuple-element.365), channel_id=1, source_target_pairs={{1,0},{2,1},{3,2},{4,3},{5,4},{6,5},{7,6},{8,7},{9,8},{10,9},{11,1... | collective-permute-start | bytes 147464 | tf_op jit(solution)/shard_map/while/body/eval_jaxpr/ppermute | solution.py:12
  1279.4 27.2 %collective-permute-start.2 = (f32[2,6,1024]{2,1,0:T(8,128)}, f32[2,6,1024]{2,1,0:T(8,128)S(1)}, u32[]{:S(2)}, u32[]{:S(2)}) collective-permute-start(f32[2,6,1024]{2,1,0:T(8,128)} %get-tuple-element.365), channel_id=1, source_target_pairs={{32,0},{64,32},{96,64},{128,96},{160,128},{192,160},{224,192},{256... | collective-permute-start | bytes 147464 | tf_op jit(solution)/shard_map/while/body/eval_jaxpr/ppermute | solution.py:12
  1341.4 24.3 %collective-permute-start.1 = (f32[2,6,1024]{2,1,0:T(8,128)}, f32[2,6,1024]{2,1,0:T(8,128)S(1)}, u32[]{:S(2)}, u32[]{:S(2)}) collective-permute-start(f32[2,6,1024]{2,1,0:T(8,128)} %get-tuple-element.363), channel_id=1, source_target_pairs={{0,1},{1,2},{2,3},{3,4},{4,5},{5,6},{6,7},{7,8},{8,9},{9,10},{10,1... | collective-permute-start | bytes 147464 | tf_op jit(solution)/shard_map/while/body/eval_jaxpr/ppermute | solution.py:12
  1362.4 27.9 %collective-permute-start.3 = (f32[2,6,1024]{2,1,0:T(8,128)}, f32[2,6,1024]{2,1,0:T(8,128)S(1)}, u32[]{:S(2)}, u32[]{:S(2)}) collective-permute-start(f32[2,6,1024]{2,1,0:T(8,128)} %get-tuple-element.365), channel_id=1, source_target_pairs={{1,0},{2,1},{3,2},{4,3},{5,4},{6,5},{7,6},{8,7},{9,8},{10,9},{11,1... | collective-permute-start | bytes 147464 | tf_op jit(solution)/shard_map/while/body/eval_jaxpr/ppermute | solution.py:12
  1364.4 26.0 %collective-permute-start.2 = (f32[2,6,1024]{2,1,0:T(8,128)}, f32[2,6,1024]{2,1,0:T(8,128)S(1)}, u32[]{:S(2)}, u32[]{:S(2)}) collective-permute-start(f32[2,6,1024]{2,1,0:T(8,128)} %get-tuple-element.365), channel_id=1, source_target_pairs={{32,0},{64,32},{96,64},{128,96},{160,128},{192,160},{224,192},{256... | collective-permute-start | bytes 147464 | tf_op jit(solution)/shard_map/while/body/eval_jaxpr/ppermute | solution.py:12
  1426.2 24.8 %collective-permute-start.1 = (f32[2,6,1024]{2,1,0:T(8,128)}, f32[2,6,1024]{2,1,0:T(8,128)S(1)}, u32[]{:S(2)}, u32[]{:S(2)}) collective-permute-start(f32[2,6,1024]{2,1,0:T(8,128)} %get-tuple-element.363), channel_id=1, source_target_pairs={{0,1},{1,2},{2,3},{3,4},{4,5},{5,6},{6,7},{7,8},{8,9},{9,10},{10,1... | collective-permute-start | bytes 147464 | tf_op jit(solution)/shard_map/while/body/eval_jaxpr/ppermute | solution.py:12
  1447.8 29.1 %collective-permute-start.3 = (f32[2,6,1024]{2,1,0:T(8,128)}, f32[2,6,1024]{2,1,0:T(8,128)S(1)}, u32[]{:S(2)}, u32[]{:S(2)}) collective-permute-start(f32[2,6,1024]{2,1,0:T(8,128)} %get-tuple-element.365), channel_id=1, source_target_pairs={{1,0},{2,1},{3,2},{4,3},{5,4},{6,5},{7,6},{8,7},{9,8},{10,9},{11,1... | collective-permute-start | bytes 147464 | tf_op jit(solution)/shard_map/while/body/eval_jaxpr/ppermute | solution.py:12
  1449.7 27.2 %collective-permute-start.2 = (f32[2,6,1024]{2,1,0:T(8,128)}, f32[2,6,1024]{2,1,0:T(8,128)S(1)}, u32[]{:S(2)}, u32[]{:S(2)}) collective-permute-start(f32[2,6,1024]{2,1,0:T(8,128)} %get-tuple-element.365), channel_id=1, source_target_pairs={{32,0},{64,32},{96,64},{128,96},{160,128},{192,160},{224,192},{256... | collective-permute-start | bytes 147464 | tf_op jit(solution)/shard_map/while/body/eval_jaxpr/ppermute | solution.py:12
  1476.9 24.7 %collective-permute-start.1 = (f32[2,6,1024]{2,1,0:T(8,128)}, f32[2,6,1024]{2,1,0:T(8,128)S(1)}, u32[]{:S(2)}, u32[]{:S(2)}) collective-permute-start(f32[2,6,1024]{2,1,0:T(8,128)} %get-tuple-element.363), channel_id=1, source_target_pairs={{0,1},{1,2},{2,3},{3,4},{4,5},{5,6},{6,7},{7,8},{8,9},{9,10},{10,1... | collective-permute-start | bytes 147464 | tf_op jit(solution)/shard_map/while/body/eval_jaxpr/ppermute | solution.py:12
  1511.3 25.1 %collective-permute-start.1 = (f32[2,6,1024]{2,1,0:T(8,128)}, f32[2,6,1024]{2,1,0:T(8,128)S(1)}, u32[]{:S(2)}, u32[]{:S(2)}) collective-permute-start(f32[2,6,1024]{2,1,0:T(8,128)} %get-tuple-element.363), channel_id=1, source_target_pairs={{0,1},{1,2},{2,3},{3,4},{4,5},{5,6},{6,7},{7,8},{8,9},{9,10},{10,1... | collective-permute-start | bytes 147464 | tf_op jit(solution)/shard_map/while/body/eval_jaxpr/ppermute | solution.py:12
  (192 other events, 2380.8 us)
where the time goes:
time: 1820 us; the launch traced here: 1800 us
  starting transfers between devices  1060 us (58%)
  waiting for transfers between devices  522 us (29%)
  loops' own time  92.5 us (5%)
  matrix products  67.6 us (4%)
  local copies, waits for them, and re-layouts  40.3 us (2%)
  other arithmetic  25.3 us (1%)
    ppermute x216, starting transfers between devices, shifted(): lax.ppermute(value, axis, [(source, source + steps) for source in range(l...  1060 us
    ppermute x216, waiting for transfers between devices, shifted(): lax.ppermute(value, axis, [(source, source + steps) for source in range(l...  522 us
    another operation x108, loops' own time, advance(): return lax.cond(active, compute, retain)  87.9 us
  transfers between devices with their start and end apart: 216, of which 56 were waited for; matrix products, arithmetic and copies ran while one was open for 4% of the time, Pallas kernels for 0%

commit v1 on v0

v1 whole, which is shorter than its diff:
```python
import functools

import jax
import jax.numpy as jnp
from jax import lax
from jax.experimental import pallas as pl
from jax.experimental.pallas import tpu as pltpu
from jax.sharding import PartitionSpec as P

COUPLING = 0.5
ROWS = 8
MESH = pl.DeviceIdType.MESH


def coefficients(code):
    flip = jnp.where(code >= 4, -1.0, 1.0).astype(jnp.float32)
    quarter = code % 4
    cos = jnp.where(quarter == 0, 1.0, jnp.where(quarter == 2, -1.0, 0.0)).astype(jnp.float32)
    sine = jnp.where(quarter == 1, 1.0, jnp.where(quarter == 3, -1.0, 0.0)).astype(jnp.float32)
    return cos, -sine * flip, sine, cos * flip


def kernel(
    nx, ny, groups, rows,
    k_hbm, s_ref, pat_ref, out_ref,
    k_ref, src_ref, sum_ref, in_x, in_y, k_sem, send_x, send_y, recv_x, recv_y,
):
    cx = lax.axis_index("gx")
    cy = lax.axis_index("gy")
    load = pltpu.make_async_copy(k_hbm, k_ref, k_sem)
    load.start()

    has = (
        (cx > 0, cy > 0),
        (cx < nx - 1, cy < ny - 1),
    )
    barrier = pltpu.get_barrier_semaphore()
    for side, (step_x, step_y) in enumerate(((-1, -1), (1, 1))):
        @pl.when(has[side][0])
        def _():
            pl.semaphore_signal(barrier, inc=1, device_id=(cx + step_x, cy), device_id_type=MESH)

        @pl.when(has[side][1])
        def _():
            pl.semaphore_signal(barrier, inc=1, device_id=(cx, cy + step_y), device_id_type=MESH)

    zero = jnp.zeros((groups, 2, rows, k_ref.shape[2]), jnp.float32)
    for side in range(2):
        @pl.when(jnp.logical_not(has[side][0]))
        def _():
            in_x[side] = zero

        @pl.when(jnp.logical_not(has[side][1]))
        def _():
            in_y[side] = zero

    for group in range(groups):
        src_ref[group] = s_ref[:, group * rows : (group + 1) * rows, :].astype(jnp.float32)

    count = sum(jnp.where(flag, 1, 0) for pair in has for flag in pair)
    pl.semaphore_wait(barrier, count)
    load.wait()

    depth = (cx + cy, nx - 1 - cx + ny - 1 - cy)
    targets = (((cx + 1, cy), (cx, cy + 1)), ((cx - 1, cy), (cx, cy - 1)))
    turns = [[coefficients(pat_ref[side, edge]) for edge in range(2)] for side in range(2)]

    def copies(side, group):
        return (
            pltpu.make_async_remote_copy(
                src_ref=sum_ref.at[side, group], dst_ref=in_x.at[side, group],
                send_sem=send_x.at[side, group], recv_sem=recv_x.at[side, group],
                device_id=targets[side][0], device_id_type=MESH,
            ),
            pltpu.make_async_remote_copy(
                src_ref=sum_ref.at[side, group], dst_ref=in_y.at[side, group],
                send_sem=send_y.at[side, group], recv_sem=recv_y.at[side, group],
                device_id=targets[side][1], device_id_type=MESH,
            ),
        )

    def advance(side, group):
        along_x, along_y = copies(side, group)

        @pl.when(has[side][0])
        def _():
            along_x.wait_recv()

        @pl.when(has[side][1])
        def _():
            along_y.wait_recv()

        (a, b, c, d), (e, f, g, h) = turns[side]
        left_re, left_im = in_x[side, group, 0], in_x[side, group, 1]
        down_re, down_im = in_y[side, group, 0], in_y[side, group, 1]
        re = (a * left_re + b * left_im) + (e * down_re + f * down_im)
        im = (c * left_re + d * left_im) + (g * down_re + h * down_im)
        first = jnp.concatenate([re, im], axis=0).astype(jnp.bfloat16)
        second = jnp.concatenate([-im, re], axis=0).astype(jnp.bfloat16)
        contract = (((1,), (side,)), ((), ()))
        product = lax.dot_general(
            first, k_ref[0], contract, preferred_element_type=jnp.float32
        ) + lax.dot_general(second, k_ref[1], contract, preferred_element_type=jnp.float32)
        width = product.shape[1]
        sum_ref[side, group] = src_ref[group] + COUPLING * product.reshape(2, rows, width)

        @pl.when(has[1 - side][0])
        def _():
            along_x.start()

        @pl.when(has[1 - side][1])
        def _():
            along_y.start()

    def section(step, carry):
        for side in range(2):
            group = step - depth[side]

            @pl.when((group >= 0) & (group < groups))
            def _():
                advance(side, group)

        return carry

    lax.fori_loop(0, nx + ny - 1 + groups - 1, section, 0)

    for group in range(groups):
        out_ref[:, group * rows : (group + 1) * rows, :] = (
            sum_ref[0, group] + sum_ref[1, group]
        ).astype(jnp.bfloat16)

    def drain(group, carry):
        for side in range(2):
            along_x, along_y = copies(side, group)

            @pl.when(has[1 - side][0])
            def _():
                along_x.wait_send()

            @pl.when(has[1 - side][1])
            def _():
                along_y.wait_send()

        return carry

    lax.fori_loop(0, groups, drain, 0)


def per_device(nx, ny, impedance, sources, pattern):
    _, _, _, count, width = sources.shape
    rows = ROWS
    groups = count // rows
    trace = (2, groups, 2, rows, width)
    vmem = pl.BlockSpec(memory_space=pltpu.VMEM)
    result = pl.pallas_call(
        functools.partial(kernel, nx, ny, groups, rows),
        out_shape=jax.ShapeDtypeStruct((2, count, width), jnp.bfloat16),
        in_specs=[
            pl.BlockSpec(memory_space=pl.ANY),
            vmem,
            pl.BlockSpec(memory_space=pltpu.SMEM),
        ],
        out_specs=vmem,
        scratch_shapes=[
            pltpu.VMEM((2, width, width), jnp.bfloat16),
            pltpu.VMEM((groups, 2, rows, width), jnp.float32),
            pltpu.VMEM(trace, jnp.float32),
            pltpu.VMEM(trace, jnp.float32),
            pltpu.VMEM(trace, jnp.float32),
            pltpu.SemaphoreType.DMA,
            pltpu.SemaphoreType.DMA((2, groups)),
            pltpu.SemaphoreType.DMA((2, groups)),
            pltpu.SemaphoreType.DMA((2, groups)),
            pltpu.SemaphoreType.DMA((2, groups)),
        ],
        compiler_params=pltpu.CompilerParams(
            collective_id=0, has_side_effects=True, vmem_limit_bytes=48 * 1024 * 1024
        ),
    )(impedance[0, 0], sources[0, 0], pattern[0, 0])
    return result[None, None]


def solution(mesh):
    in_specs = (
        P("gx", "gy", None, None, None),
        P("gx", "gy", None, None, None),
        P("gx", "gy", None, None),
    )
    out_specs = P("gx", "gy", None, None, None)
    body = functools.partial(per_device, mesh.shape["gx"], mesh.shape["gy"])
    return jax.shard_map(body, mesh=mesh, in_specs=in_specs, out_specs=out_specs, check_vma=False)
```

time: 1820 us -> 365 us (0.20)
  starting transfers between devices: 1060 us -> 0 us
  waiting for transfers between devices: 522 us -> 0 us
  Pallas kernels: 0 us -> 360 us
  loops' own time: 92.5 us -> 0 us
  matrix products: 67.6 us -> 0 us
  local copies, waits for them, and re-layouts: 40.3 us -> 4.47 us
  other arithmetic: 25.3 us -> 0 us
    ppermute x216 -> x0, starting transfers between devices: 1060 us -> none  [shifted(): lax.ppermute(value, axis, [(source, source + steps) for source in range(l...]
    ppermute x216 -> x0, waiting for transfers between devices: 522 us -> none  [shifted(): lax.ppermute(value, axis, [(source, source + steps) for source in range(l...]
    pallas_call x0 -> x1, Pallas kernels: none -> 360 us  [per_device(): pl.pallas_call(functools.partial(kernel, nx, ny, groups, rows), out_shape...]
    another operation x109 -> x0, loops' own time: 92.5 us -> none  [the longest x108 87.9 us: advance(): return lax.cond(active, compute, retain)]
    dot_general x32 -> x0, matrix products: 67.6 us -> none  [the longest x16 33.8 us: apply_operator(): lax.dot_general(blended, operator_block[0], contract, preferred_element_t...]
    add x32 -> x0, other arithmetic: 24.3 us -> none  [the longest x16 23.8 us: apply_operator(): source_block.astype(jnp.float32) + COUPLING * jnp.stack([out_re, out_im])]
    slice x16 -> x0, local copies, waits for them, and re-layouts: 22.7 us -> none  [apply_operator(): left_re, left_im = rotate(edge_codes[0], left_in[0], left_in[1])]
  transfers between devices with their start and end apart: 216 -> 0, of which waited for: 56 -> 0; matrix products, arithmetic and copies ran while one was open for 4% -> 0% of each run, Pallas kernels for 0% -> 0%
where the time goes in v1:
time: 365 us
  Pallas kernels  360 us (99%)
  local copies, waits for them, and re-layouts  4.47 us (1%)
    pallas_call x1, Pallas kernels, per_device(): pl.pallas_call(functools.partial(kernel, nx, ny, groups, rows), out_shape...  360 us

profile of v1, /device:TPU:1, one launch (start us, length us, event | category | flops | bytes accessed | tf_op | source)
XLA Modules:
  0.0 364.5 jit_solution(5024969676989142789)
XLA Ops:
  0.0 0.0 copy-start
  0.0 2.2 copy-done
  2.2 0.0 copy-start.1
  2.2 0.9 copy-done.1
  3.1 0.0 copy-start.2
  3.1 0.7 copy-done.2
  3.8 360.0 %shard_map.37 = bf16[2,48,1024]{2,1,0:T(8,128)(2,1)S(1)} custom-call(bf16[2,1024,1024]{2,1,0:T(8,128)(2,1)S(1)} %bitcast.4, bf16[2,48,1024]{2,1,0:T(8,128)(2,1)S(1)} %bitcast.6, s32[2,2]{1,0:T(2,128)S(1)} %bitcast.7), custom_call_target="tpu_custom_call" | custom-call | tf_op jit(solution)/shard_map/pallas_call | solution.py:155
  363.8 0.7 copy.5
Async XLA Ops:
  0.0 2.2 copy-start
  2.2 0.9 copy-start.1
  3.1 0.7 copy-start.2
